TPU v7x, 512 devices: a whole 4x4x16 slice. The times are simulated.
512 devices in a mesh: seq: 64 (over y, z), mp: 8 (over x, core).
Axes of the slice: x: 4, y: 4, z: 16, core: 2. Of those that a mesh axis runs over, the one named last changes fastest.
Arguments:
- projections: bfloat16 [16384, 6144], P('seq', 'mp'), may hold values from -80 to 80
- qk_gain: float32 [2, 128], replicated, may hold values from 0.1 to 1.9
- clusters: int32 [16, 16384, 1], P('mp', 'seq'), may hold values from 0 to 63; in each aligned block of 256 rows (0 to 255, 256 to 511, ..., all dimensions but the last counted through in order) at most 10 rows name the same one
- d_out: bfloat16 [16384, 4096], P('seq'), may hold values from -64 to 64
- w_out: bfloat16 [4096, 2048], P(None, 'mp'), may hold values from -0.125 to 0.125
Outputs:
- d_projections: bfloat16 [16384, 6144], P('seq', 'mp')
- d_w_out: float32 [4096, 2048], P('seq', 'mp')
Inputs may be any that keep to these rules, and one draw needn't show every extreme that they name: `clusters`: for each head, among the 256 tokens of one index of seq no cluster holds more than 10 tokens, and some cluster holds exactly 10 of them for some head and index.
All inputs are finite; a program needn't handle non-finite values.
Results may differ from a plain program's by a relative error of at most 0.009.
Values may be sent and summed in bfloat16 or wider, within the bound.
A program may use at most 64 MiB of HBM per device.

v0:
```python
import jax
import jax.numpy as jnp
from jax import lax
from jax.sharding import PartitionSpec as P

EPSILON = 1e-06


def normalize(raw):
    data = raw.astype(jnp.float32)
    inverse = lax.rsqrt(jnp.mean(data * data, axis=-1, keepdims=True) + EPSILON)
    return (data * inverse, inverse)


def norm_back(unit, inverse, gain, upstream):
    scaled = upstream * gain
    return inverse * (scaled - unit * jnp.mean(scaled * unit, axis=-1, keepdims=True))


def owner_forward(query_hat, key_hat, values, live):
    scale = query_hat.shape[-1] ** (-0.5)
    scores = (
        jnp.einsum("hqe,hke->hqk", query_hat, key_hat, preferred_element_type=jnp.float32) * scale
    )
    expo = jnp.exp(scores) * live[:, None, :]
    denominator = jnp.sum(expo, axis=-1, keepdims=True) + (1.0 - live)[:, :, None]
    probs = expo / denominator
    probs_low = probs.astype(jnp.bfloat16)
    output = jnp.einsum("hqk,hke->hqe", probs_low, values, preferred_element_type=jnp.float32)
    return (probs, probs_low, output)


def owner_backward(query_hat, key_hat, values, grad_out, probs, probs_low):
    scale = query_hat.shape[-1] ** (-0.5)
    grad_probs = jnp.einsum("hqe,hke->hqk", grad_out, values, preferred_element_type=jnp.float32)
    row_dot = jnp.sum(probs * grad_probs, axis=-1, keepdims=True)
    grad_scores = (probs * (grad_probs - row_dot) * scale).astype(jnp.bfloat16)
    grad_query = jnp.einsum(
        "hqk,hke->hqe", grad_scores, key_hat, preferred_element_type=jnp.float32
    )
    grad_key = jnp.einsum(
        "hqk,hqe->hke", grad_scores, query_hat, preferred_element_type=jnp.float32
    )
    grad_value = jnp.einsum("hqk,hqe->hke", probs_low, grad_out, preferred_element_type=jnp.float32)
    return jnp.concatenate([grad_query, grad_key, grad_value], axis=-1)


def per_device(projections, qk_gain, clusters, d_out, w_out):
    tokens_here = projections.shape[0]
    head_size = qk_gain.shape[1]
    heads_here = clusters.shape[0]
    owners = lax.axis_size("seq")
    capacity = max(2, 5 * tokens_here // (2 * owners))
    slot_count = owners * capacity
    split_proj = projections.reshape(tokens_here, heads_here, 3, head_size)
    query_unit, query_inverse = normalize(split_proj[:, :, 0])
    key_unit, key_inverse = normalize(split_proj[:, :, 1])
    query_hat = (query_unit * qk_gain[0]).astype(jnp.bfloat16)
    key_hat = (key_unit * qk_gain[1]).astype(jnp.bfloat16)
    values = split_proj[:, :, 2]
    grad_attention = jnp.dot(d_out, w_out, preferred_element_type=jnp.float32).astype(jnp.bfloat16)
    grad_attention = grad_attention.reshape(tokens_here, heads_here, head_size)
    ident = clusters[:, :, 0]
    member = (ident[:, :, None] == jnp.arange(owners, dtype=jnp.int32)[None, None, :]).astype(
        jnp.int32
    )
    rank = jnp.sum((jnp.cumsum(member, axis=1) - 1) * member, axis=-1)
    target = ident * capacity + rank
    chooser = (target[:, :, None] == jnp.arange(slot_count, dtype=jnp.int32)[None, None, :]).astype(
        jnp.bfloat16
    )
    live_flags = jnp.sum(chooser, axis=1).reshape(heads_here, owners, capacity)

    def pack(payload):
        packed = jnp.einsum("hts,thw->hsw", chooser, payload, preferred_element_type=jnp.float32)
        return packed.astype(jnp.bfloat16).reshape(heads_here, owners, capacity, -1)

    def unpack(arrived):
        flat_rows = arrived.reshape(heads_here, slot_count, -1)
        return jnp.einsum("hts,hsw->thw", chooser, flat_rows, preferred_element_type=jnp.float32)

    payload = jnp.concatenate([query_hat, key_hat, values], axis=-1)
    packed, flags = (
        lax.all_to_all(pack(payload), "seq", split_axis=1, concat_axis=1, tiled=True),
        lax.all_to_all(live_flags, "seq", split_axis=1, concat_axis=1, tiled=True),
    )
    rows_all = packed.reshape(heads_here, slot_count, 3 * head_size)
    live = flags.reshape(heads_here, slot_count).astype(jnp.float32)
    owner_query = rows_all[:, :, :head_size]
    owner_key = rows_all[:, :, head_size : 2 * head_size]
    owner_value = rows_all[:, :, 2 * head_size :]
    probs, probs_low, output = owner_forward(owner_query, owner_key, owner_value, live)
    output_low = output.astype(jnp.bfloat16).reshape(heads_here, owners, capacity, head_size)
    output_home = lax.all_to_all(output_low, "seq", split_axis=1, concat_axis=1, tiled=True)
    grad_arrived = lax.all_to_all(
        pack(grad_attention), "seq", split_axis=1, concat_axis=1, tiled=True
    )
    grad_rows = grad_arrived.reshape(heads_here, slot_count, head_size)
    grads = owner_backward(owner_query, owner_key, owner_value, grad_rows, probs, probs_low)
    grads_low = grads.astype(jnp.bfloat16).reshape(heads_here, owners, capacity, 3 * head_size)
    grads_back = lax.all_to_all(grads_low, "seq", split_axis=1, concat_axis=1, tiled=True)
    results = jnp.concatenate([unpack(output_home), unpack(grads_back)], axis=-1)
    attention = (
        results[:, :, :head_size].astype(jnp.bfloat16).reshape(tokens_here, heads_here * head_size)
    )
    grad_query = norm_back(
        query_unit, query_inverse, qk_gain[0], results[:, :, head_size : 2 * head_size]
    )
    grad_key = norm_back(
        key_unit, key_inverse, qk_gain[1], results[:, :, 2 * head_size : 3 * head_size]
    )
    grad_value = results[:, :, 3 * head_size :]
    d_projections = jnp.stack([grad_query, grad_key, grad_value], axis=2).astype(jnp.bfloat16)
    d_projections = d_projections.reshape(tokens_here, heads_here * 3 * head_size)
    summed = lax.psum_scatter(
        lax.dot_general(
            d_out, attention, (((0,), (0,)), ((), ())), preferred_element_type=jnp.float32
        ),
        "seq",
        scatter_dimension=0,
        tiled=True,
    )
    d_w_out = summed * (tokens_here * owners) ** (-0.5)
    return (d_projections, d_w_out)


def solution(mesh):
    in_specs = (P("seq", "mp"), P(), P("mp", "seq", None), P("seq", None), P(None, "mp"))
    out_specs = (P("seq", "mp"), P("seq", "mp"))
    return jax.shard_map(
        per_device, mesh=mesh, in_specs=in_specs, out_specs=out_specs, check_vma=False
    )
```

profile of v0, /device:TPU:4, one launch (start us, length us, event | category | flops | bytes accessed | tf_op | source)
XLA Modules:
  0.0 857.4 jit_solution(3377365199841298431)
XLA Ops:
  8.7 1.2 reduce-window.6
  12.0 18.7 %all-to-all-start.1 = ((bf16[2,64,10]{2,0,1:T(2,128)(2,1)}), bf16[2,64,10]{2,0,1:T(2,128)(2,1)S(1)}, u32[]{:S(2)}, u32[]{:S(2)}) async-start(bf16[2,64,10]{2,0,1:T(2,128)(2,1)} %copy.81), calls=%async_computation.1 | async-start | bytes 65536 | tf_op jit(solution)/shard_map/all_to_all | solution.py:85
  31.5 1.2 copy.72
  34.3 2.0 copy.78
  36.3 8.8 %all-to-all-done.1 = bf16[2,64,10]{2,0,1:T(2,128)(2,1)S(1)} async-done(((bf16[2,64,10]{2,0,1:T(2,128)(2,1)}), bf16[2,64,10]{2,0,1:T(2,128)(2,1)S(1)}, u32[]{:S(2)}, u32[]{:S(2)}) %all-to-all-start.1) | async-done | bytes 2592 | tf_op jit(solution)/shard_map/all_to_all | solution.py:85
  45.1 6.3 all-to-all-start
  51.8 50.3 %all-to-all-done = bf16[2,64,10,384]{3,0,2,1:T(2,128)(2,1)S(1)} async-done(((bf16[2,64,10,384]{3,0,2,1:T(2,128)(2,1)}), bf16[2,64,10,384]{3,0,2,1:T(2,128)(2,1)S(1)}, u32[]{:S(2)}, u32[]{:S(2)}) %all-to-all-start) | async-done | bytes 983072 | tf_op jit(solution)/shard_map/all_to_all | solution.py:84
  103.7 1.1 convolution_convert_fusion.1
  105.4 1.0 copy.98
  106.5 6.6 all-to-all-start.4
  113.3 2.5 convolution_convert_fusion.4
  115.8 20.7 %all-to-all-done.4 = bf16[2,64,10,128]{3,0,2,1:T(2,128)(2,1)S(1)} async-done(((bf16[2,64,10,128]{3,0,2,1:T(2,128)(2,1)}), bf16[2,64,10,128]{3,0,2,1:T(2,128)(2,1)S(1)}, u32[]{:S(2)}, u32[]{:S(2)}) %all-to-all-start.4) | async-done | bytes 327712 | tf_op jit(solution)/shard_map/all_to_all | solution.py:94
  137.0 2.7 convolution_bitcast_fusion
  139.7 5.6 copy.108
  146.2 30.7 %all_to_all.25 = bf16[2,64,10,128]{3,0,2,1:T(2,128)(2,1)S(1)} all-to-all(bf16[2,64,10,128]{3,0,2,1:T(2,128)(2,1)S(1)} %bitcast.75), channel_id=1, replica_groups=mesh['seq'=64,'mp'=8] {'seq'}, dimensions={1} | all-to-all | bytes 655360 | tf_op jit(solution)/shard_map/all_to_all | solution.py:95
  176.9 2.8 convolution_convert_fusion.2
  180.1 2.3 fusion.47
  182.4 7.3 fusion.18
  190.1 7.2 fusion.21
  197.6 1.2 pad_maximum_fusion
  198.8 59.2 %all_to_all.26 = bf16[2,64,10,384]{3,0,2,1:T(2,128)(2,1)S(1)} all-to-all(bf16[2,64,10,384]{3,0,2,1:T(2,128)(2,1)S(1)} %pad_maximum_fusion), channel_id=1, replica_groups=mesh['seq'=64,'mp'=8] {'seq'}, dimensions={1} | all-to-all | bytes 1966080 | tf_op jit(solution)/shard_map/all_to_all | solution.py:101
  259.6 0.9 copy.100
  260.6 588.3 %reduce-scatter.4.cloned.1.call-done = f32[64,256]{1,0:T(8,128)} async-done(((f32[4096,256]{1,0:T(8,128)}), f32[64,256]{1,0:T(8,128)}) %reduce-scatter.4.cloned.1.call-update) | async-done | bytes 65552
  848.9 0.9 copy.109
  (60 shorter events, 13.3 us)
Async XLA Ops:
  7.2 106.2 %copy-start = (bf16[256,4096]{1,0:T(8,128)(2,1)S(1)}, bf16[256,4096]{1,0:T(8,128)(2,1)}, u32[]{:S(2)}) copy-start(bf16[256,4096]{1,0:T(8,128)(2,1)} %param.8) | copy-start | bytes 6291460
  12.0 33.1 %all-to-all-start.1 = ((bf16[2,64,10]{2,0,1:T(2,128)(2,1)}), bf16[2,64,10]{2,0,1:T(2,128)(2,1)S(1)}, u32[]{:S(2)}, u32[]{:S(2)}) async-start(bf16[2,64,10]{2,0,1:T(2,128)(2,1)} %copy.81), calls=%async_computation.1 | async-start | bytes 65536 | tf_op jit(solution)/shard_map/all_to_all | solution.py:85
  45.1 57.0 %all-to-all-start = ((bf16[2,64,10,384]{3,0,2,1:T(2,128)(2,1)}), bf16[2,64,10,384]{3,0,2,1:T(2,128)(2,1)S(1)}, u32[]{:S(2)}, u32[]{:S(2)}) async-start(bf16[2,64,10,384]{3,0,2,1:T(2,128)(2,1)} %bitcast.72), calls=%async_computation | async-start | bytes 1966080 | tf_op jit(solution)/shard_map/all_to_all | solution.py:84
  102.8 0.9 copy-start.3
  102.8 0.9 copy-start.4
  102.8 2.0 copy-start.1
  103.6 1.8 copy-start.6
  106.5 30.1 %all-to-all-start.4 = ((bf16[2,64,10,128]{3,0,2,1:T(2,128)(2,1)}), bf16[2,64,10,128]{3,0,2,1:T(2,128)(2,1)S(1)}, u32[]{:S(2)}, u32[]{:S(2)}) async-start(bf16[2,64,10,128]{3,0,2,1:T(2,128)(2,1)} %bitcast.24), calls=%async_computation.4 | async-start | bytes 655360 | tf_op jit(solution)/shard_map/all_to_all | solution.py:94
  113.1 735.8 %reduce-scatter.4.cloned.1.call-start = ((), (), s32[]{:S(2)}) async-start(), calls=%async_computation.6 | async-start | bytes 4259840
  176.9 3.2 copy-start.2
  179.7 2.7 copy-start.5
Sparse Core Ops, SparseCore 0:
  145.5 703.3 reduce-scatter.3
where the time goes:
time: 858 us; the launch traced here: 857 us
  waiting for transfers between devices  668 us (78%)
  blocking collectives  89.9 us (10%)
  starting transfers between devices  31.8 us (4%)
  matrix products  29 us (3%)
  local copies, waits for them, and re-layouts  18.6 us (2%)
  between operations  14.4 us (2%)
    unnamed x2, waiting for transfers between devices  588 us
    all_to_all x1, blocking collectives, per_device(): lax.all_to_all(grads_low, 'seq', split_axis=1, concat_axis=1, tiled=True)  59.2 us
    all_to_all x1, waiting for transfers between devices, per_device(): lax.all_to_all(pack(payload), 'seq', split_axis=1, concat_axis=1, tiled=T...  50.3 us
    all_to_all x1, blocking collectives, per_device(): lax.all_to_all(pack(grad_attention), 'seq', split_axis=1, concat_axis=1,...  30.7 us
    all_to_all x1, waiting for transfers between devices, per_device(): lax.all_to_all(output_low, 'seq', split_axis=1, concat_axis=1, tiled=True)  20.7 us
    all_to_all x1, starting transfers between devices, per_device(): lax.all_to_all(live_flags, 'seq', split_axis=1, concat_axis=1, tiled=True)  18.7 us
  transfers between devices with their start and end apart: 4, of which 4 were waited for; matrix products, arithmetic and copies ran while one was open for 4% of the time, Pallas kernels for 0%

commit v1 on v0

v1 whole, which is shorter than its diff:
```python
import functools

import jax
import jax.numpy as jnp
from jax import lax
from jax.experimental import pallas as pl
from jax.experimental.pallas import tpu as pltpu
from jax.sharding import PartitionSpec as P

EPSILON = 1e-06
HS = 128
HEADS = 2
CAP = 10
MAIN = 8
DEAD = 1024.0
TILE = 16
F32 = jnp.float32
BF16 = jnp.bfloat16

MAIN_ROW = (0, 32, 48, 64)
REST_ROW = 16
ROWS = 80
FIRST = 32


def dot(a, b, dims):
    return lax.dot_general(a, b, (dims, ((), ())), preferred_element_type=F32)


def normalize(raw):
    data = raw.astype(F32)
    inverse = lax.rsqrt(jnp.mean(data * data, axis=-1, keepdims=True) + EPSILON)
    return data * inverse, inverse


def norm_back(unit, inverse, gain, upstream):
    scaled = upstream * gain
    return inverse * (scaled - unit * jnp.mean(scaled * unit, axis=-1, keepdims=True))


def kernel(ny, nz, proj, gain, ids_row, ids_col, d_out, w_out, d_proj, d_w,
           sent, arrived, back1, back2, home1, home2, rest, d_cols, d_cols_t,
           att, att_all, part, part_all, qs, ks, vs, gs, low, grad_low,
           chooser_t, sems):
    n = ny * nz
    tokens = proj.shape[0]
    slots = n * CAP
    width = d_out.shape[1] // ny
    me = lax.axis_index("seq")
    my_y, my_z = me // nz, me % nz

    def other(step):
        j, dy = step // ny, step % ny
        dz = jnp.where(j % 2 == 1, (j + 1) // 2, nz - j // 2)
        return ((my_y + dy) % ny) * nz + (my_z + dz) % nz

    def remote(src, dst, number, target):
        return pltpu.make_async_remote_copy(
            src_ref=src, dst_ref=dst, send_sem=sems.at[2 * number],
            recv_sem=sems.at[2 * number + 1], device_id={"seq": target},
            device_id_type=pl.DeviceIdType.MESH)

    def wait_sent(ref, number):
        pltpu.make_async_copy(ref, ref, sems.at[2 * number]).wait()

    def wait_arrived(ref, number):
        pltpu.make_async_copy(ref, ref, sems.at[2 * number + 1]).wait()

    barrier = pltpu.get_barrier_semaphore()

    @pl.loop(1, n)
    def _(step):
        pl.semaphore_signal(barrier, inc=1, device_id={"seq": other(step)},
                            device_id_type=pl.DeviceIdType.MESH)

    grad_att = dot(d_out[...], w_out[...], ((1,), (0,))).astype(BF16)
    ones = jnp.ones((tokens, HS), BF16)
    packed = []
    for h in range(HEADS):
        first = h * 3 * HS
        q_unit, _ = normalize(proj[:, first:first + HS])
        k_unit, _ = normalize(proj[:, first + HS:first + 2 * HS])
        payload = jnp.concatenate(
            [(q_unit * gain[0:1, :]).astype(BF16), (k_unit * gain[1:2, :]).astype(BF16),
             proj[:, first + 2 * HS:first + 3 * HS], grad_att[:, h * HS:(h + 1) * HS], ones], axis=1)
        row, col = ids_row[h], ids_col[h]
        same = row == col
        t0 = lax.broadcasted_iota(jnp.int32, (tokens, tokens), 0)
        t1 = lax.broadcasted_iota(jnp.int32, (tokens, tokens), 1)
        rank_row = jnp.sum(jnp.where(same & (t0 < t1), 1.0, 0.0), axis=0, keepdims=True).astype(jnp.int32)
        rank_col = jnp.sum(jnp.where(same & (t1 < t0), 1.0, 0.0), axis=1, keepdims=True).astype(jnp.int32)

        def place(ids, rank):
            return jnp.where(rank < MAIN, ids * MAIN + rank, n * MAIN + (rank - MAIN) * n + ids)

        chooser = jnp.where(
            place(row, rank_row) == lax.broadcasted_iota(jnp.int32, (slots, tokens), 0), 1.0, 0.0).astype(BF16)
        chooser_t[h] = jnp.where(
            place(col, rank_col) == lax.broadcasted_iota(jnp.int32, (tokens, slots), 1), 1.0, 0.0).astype(BF16)
        rows = dot(chooser, payload, ((1,), (0,)))
        live = rows[:, 4 * HS:]
        packed.append([rows[:, :HS], rows[:, HS:2 * HS],
                       rows[:, 2 * HS:3 * HS] + (1.0 - live) * DEAD, rows[:, 3 * HS:4 * HS]])

    def main_tile(parts, c):
        both = [parts[h][c][:n * MAIN].reshape(n, MAIN, HS) for h in range(HEADS)]
        return jnp.concatenate(both, axis=1).astype(BF16)

    def rest_tile(parts):
        for h in range(HEADS):
            for c in range(4):
                for r in range(CAP - MAIN):
                    start = n * (MAIN + r)
                    rest[pl.ds(c * 4 + h * 2 + r, n, stride=TILE), :] = parts[h][c][start:start + n]
        return rest[...].reshape(n, TILE, HS).astype(BF16)

    def slots_of(main, c, h):
        pieces = [main.astype(F32)[:, h * MAIN:(h + 1) * MAIN].reshape(n * MAIN, HS)]
        for r in range(CAP - MAIN):
            pieces.append(rest[pl.ds(c * 4 + h * 2 + r, n, stride=TILE), :])
        return jnp.concatenate(pieces, axis=0)

    for c in range(4):
        sent[:, MAIN_ROW[c]:MAIN_ROW[c] + TILE] = main_tile(packed, c)
    sent[:, REST_ROW:REST_ROW + TILE] = rest_tile(packed)

    pl.semaphore_wait(barrier, n - 1)

    @pl.loop(1, n)
    def _(step):
        target = other(step)
        remote(sent.at[target], arrived.at[me], 0, target).start()

    for dy in range(1, ny):
        to_y = (my_y + dy) % ny
        start = pl.multiple_of(to_y * width, width)
        remote(d_out.at[:, pl.ds(start, width)], d_cols.at[my_y], 1, to_y * nz + my_z).start()
    own = pl.multiple_of(my_y * width, width)
    d_cols[my_y] = d_out[:, pl.ds(own, width)]
    arrived[me] = sent[me]

    wait_arrived(arrived.at[pl.ds(0, n - 1)], 0)

    rest[...] = arrived[:, REST_ROW:REST_ROW + TILE].astype(F32).reshape(n * TILE, HS)
    scale = HS ** -0.5
    results = []
    for h in range(HEADS):
        for c, ref in enumerate((qs, ks, vs, gs)):
            rows = slots_of(arrived[:, MAIN_ROW[c]:MAIN_ROW[c] + TILE], c, h)
            if c == 2:
                live = jnp.where(rows < DEAD / 2, 1.0, 0.0)[:, 0:1]
                rows = jnp.where(rows < DEAD / 2, rows, 0.0)
            ref[...] = rows.astype(BF16)
        out_t, grad_q_t = [], []
        for start in range(0, slots, 2 * HS):
            size = min(2 * HS, slots - start)
            block = slice(start, start + size)
            scores = dot(ks[...], qs[block], ((1,), (1,))) * scale
            expo = jnp.exp(scores) * live
            total = jnp.sum(expo, axis=0, keepdims=True)
            total = jnp.where(total == 0.0, 1.0, total)
            probs = expo / total
            probs_low = probs.astype(BF16)
            grad_probs = dot(vs[...], gs[block], ((1,), (1,)))
            row_dot = jnp.sum(probs * grad_probs, axis=0, keepdims=True)
            grad_scores = (probs * (grad_probs - row_dot) * scale).astype(BF16)
            low[:, block] = probs_low
            grad_low[:, block] = grad_scores
            out_t.append(dot(vs[...], probs_low, ((0,), (0,))))
            grad_q_t.append(dot(ks[...], grad_scores, ((0,), (0,))))
        out = jnp.concatenate(out_t, axis=1).T
        grad_q = jnp.concatenate(grad_q_t, axis=1).T
        grad_k = dot(grad_low[...], qs[...], ((1,), (0,)))
        grad_v = dot(low[...], gs[...], ((1,), (0,)))
        results.append([out, grad_q, grad_k, grad_v])
    back1[:, REST_ROW:REST_ROW + TILE] = rest_tile(results)
    back1[:, 0:TILE] = main_tile(results, 0)
    for c in range(1, 4):
        start = MAIN_ROW[c] - FIRST
        back2[:, start:start + TILE] = main_tile(results, c)

    @pl.loop(1, n)
    def _(step):
        target = other(step)
        remote(back1.at[target], home1.at[me], 2, target).start()

    @pl.loop(1, n)
    def _(step):
        target = other(step)
        remote(back2.at[target], home2.at[me], 3, target).start()

    home1[me] = back1[me]
    home2[me] = back2[me]

    wait_arrived(d_cols.at[pl.ds(0, ny - 1)], 1)
    for y in range(ny):
        d_cols_t[:, y * tokens:(y + 1) * tokens] = d_cols[y].T

    wait_arrived(home1.at[pl.ds(0, n - 1)], 2)
    rest[...] = home1[:, REST_ROW:REST_ROW + TILE].astype(F32).reshape(n * TILE, HS)
    for h in range(HEADS):
        rows = slots_of(home1[:, 0:TILE], 0, h).astype(BF16)
        att[:, h * HS:(h + 1) * HS] = dot(chooser_t[h], rows, ((1,), (0,))).astype(BF16)
    for dy in range(1, ny):
        to_y = (my_y + dy) % ny
        remote(att, att_all.at[my_y], 4, to_y * nz + my_z).start()
    att_all[my_y] = att[...]
    wait_arrived(att_all.at[pl.ds(0, ny - 1)], 4)
    gathered = att_all[...].reshape(ny * tokens, HEADS * HS)
    rows_z = width // nz
    part[...] = dot(d_cols_t[...], gathered, ((1,), (0,))).astype(BF16).reshape(nz, rows_z, HEADS * HS)

    @pl.loop(1, nz)
    def _(step):
        to_z = (my_z + jnp.where(step % 2 == 1, (step + 1) // 2, nz - step // 2)) % nz
        remote(part.at[to_z], part_all.at[my_z], 5, my_y * nz + to_z).start()

    part_all[my_z] = part[my_z]

    wait_arrived(home2.at[pl.ds(0, n - 1)], 3)
    for h in range(HEADS):
        grads = []
        for c in range(1, 4):
            start = MAIN_ROW[c] - FIRST
            grads.append(slots_of(home2[:, start:start + TILE], c, h).astype(BF16))
        found = dot(chooser_t[h], jnp.concatenate(grads, axis=1), ((1,), (0,)))
        first = h * 3 * HS
        for c in range(2):
            unit, inverse = normalize(proj[:, first + c * HS:first + (c + 1) * HS])
            d_proj[:, first + c * HS:first + (c + 1) * HS] = norm_back(
                unit, inverse, gain[c:c + 1, :], found[:, c * HS:(c + 1) * HS]).astype(BF16)
        d_proj[:, first + 2 * HS:first + 3 * HS] = found[:, 2 * HS:].astype(BF16)

    wait_arrived(part_all.at[pl.ds(0, nz - 1)], 5)
    total = part_all[0].astype(F32)
    for z in range(1, nz):
        total = total + part_all[z].astype(F32)
    d_w[...] = total * (tokens * n) ** -0.5

    wait_sent(sent.at[pl.ds(0, n - 1)], 0)
    wait_sent(d_cols.at[pl.ds(0, ny - 1)], 1)
    wait_sent(back1.at[pl.ds(0, n - 1)], 2)
    wait_sent(back2.at[pl.ds(0, n - 1)], 3)
    wait_sent(att_all.at[pl.ds(0, ny - 1)], 4)
    wait_sent(part.at[pl.ds(0, nz - 1)], 5)


def per_device(ny, projections, qk_gain, clusters, d_out, w_out):
    tokens = projections.shape[0]
    n = lax.axis_size("seq")
    nz = n // ny
    slots = n * CAP
    width = d_out.shape[1] // ny
    columns = HEADS * HS
    vmem = pltpu.VMEM
    scratch = [
        vmem((n, ROWS, HS), BF16), vmem((n, ROWS, HS), BF16),
        vmem((n, FIRST, HS), BF16), vmem((n, ROWS - FIRST, HS), BF16),
        vmem((n, FIRST, HS), BF16), vmem((n, ROWS - FIRST, HS), BF16),
        vmem((n * TILE, HS), F32),
        vmem((ny, tokens, width), BF16), vmem((width, ny * tokens), BF16),
        vmem((tokens, columns), BF16), vmem((ny, tokens, columns), BF16),
        vmem((nz, width // nz, columns), BF16), vmem((nz, width // nz, columns), BF16),
        vmem((slots, HS), BF16), vmem((slots, HS), BF16), vmem((slots, HS), BF16), vmem((slots, HS), BF16),
        vmem((slots, slots), BF16), vmem((slots, slots), BF16),
        vmem((HEADS, tokens, slots), BF16),
        pltpu.SemaphoreType.DMA((12,)),
    ]
    whole = pl.BlockSpec(memory_space=pltpu.VMEM)
    return pl.pallas_call(
        functools.partial(kernel, ny, nz),
        out_shape=(jax.ShapeDtypeStruct(projections.shape, BF16),
                   jax.ShapeDtypeStruct((width // nz, columns), F32)),
        in_specs=[whole] * 6,
        out_specs=(whole, whole),
        scratch_shapes=scratch,
        compiler_params=pltpu.CompilerParams(
            collective_id=0, has_side_effects=True, vmem_limit_bytes=56 * 1024 * 1024),
    )(projections, qk_gain, clusters.reshape(HEADS, 1, tokens), clusters, d_out, w_out)


def solution(mesh):
    ny = 4 if mesh.shape["seq"] == 64 else 2
    in_specs = (P("seq", "mp"), P(), P("mp", "seq", None), P("seq", None), P(None, "mp"))
    out_specs = (P("seq", "mp"), P("seq", "mp"))
    return jax.shard_map(functools.partial(per_device, ny), mesh=mesh, in_specs=in_specs,
                         out_specs=out_specs, check_vma=False)
```

time: 858 us -> 172 us (0.20)
  the two profiles are of different devices: /device:TPU:4 before, /device:TPU:40 now
where the time goes in v1:
time: 172 us
  Pallas kernels  167 us (97%)
  local copies, waits for them, and re-layouts  4.78 us (3%)
    pallas_call x1, Pallas kernels, per_device(): pl.pallas_call(functools.partial(kernel, ny, nz), out_shape=(jax.ShapeDty...  167 us
    unnamed x3, local copies, waits for them, and re-layouts  4.78 us

profile of v1, /device:TPU:40, one launch (start us, length us, event | category | flops | bytes accessed | tf_op | source)
XLA Modules:
  0.0 172.0 jit_solution(3627222261301118808)
XLA Ops:
  0.6 1.5 copy.7.ids_col
  2.2 166.6 %shard_map.68 = (bf16[256,768]{1,0:T(8,128)(2,1)}, f32[64,256]{1,0:T(8,128)}) custom-call(bf16[256,768]{1,0:T(8,128)(2,1)} %proj.1, f32[2,128]{1,0:T(2,128)} %gain.1, s32[2,1,256]{2,1,0:T(1,128)} %bitcast.1, s32[2,256,1]{2,1,0:T(8,128)} %copy.7.ids_col, bf16[256,4096]{1,0:T(8,128)(2,1)} %d_out.1, bf16[4096,256]{1,0:T(8,128)(2,1)} %w_out.1), custom_call_target="tpu_custom_call" | custom-call | tf_op jit(solution)/shard_map/pallas_call | solution.py:270
  168.8 1.8 %copy.10 = bf16[256,768]{1,0:T(8,128)(2,1)} copy(bf16[256,768]{1,0:T(8,128)(2,1)} %get-tuple-element.4) | data formatting | bytes 786432
  170.5 1.5 copy.11

commit v2 on v1

--- a/solution.py
+++ b/solution.py
@@ -38,40 +38,62 @@
     return inverse * (scaled - unit * jnp.mean(scaled * unit, axis=-1, keepdims=True))
 
 
-def kernel(ny, nz, proj, gain, ids_row, ids_col, d_out, w_out, d_proj, d_w,
-           sent, arrived, back1, back2, home1, home2, rest, d_cols, d_cols_t,
-           att, att_all, part, part_all, qs, ks, vs, gs, low, grad_low,
-           chooser_t, sems):
+def write_out(d_proj, d_w, d_proj_out, d_w_out):
+    d_proj_out[...] = d_proj[...]
+    d_w_out[...] = d_w[...]
+
+
+def kernel(ny, nz, gain, ids_row, proj_in, d_out_in, w_out_in, d_proj, d_w,
+           proj, d_out, w_out, sent, arrived, back1, back2, home1, home2, rest, d_cols, d_cols_t,
+           att, att_all, part, out_r, out_l, in_r, in_l, qs, ks, vs, gs, low, grad_low,
+           codes, chooser_t, in_sems, sems, ring_sems):
     n = ny * nz
     tokens = proj.shape[0]
     slots = n * CAP
     width = d_out.shape[1] // ny
+    rows_z = width // nz
     me = lax.axis_index("seq")
-    my_y, my_z = me // nz, me % nz
+    my_y, my_z = lax.div(me, nz), lax.rem(me, nz)
 
     def other(step):
-        j, dy = step // ny, step % ny
-        dz = jnp.where(j % 2 == 1, (j + 1) // 2, nz - j // 2)
-        return ((my_y + dy) % ny) * nz + (my_z + dz) % nz
+        step = n - step
+        j, dy = lax.div(step, ny), lax.rem(step, ny)
+        dz = jnp.where(lax.rem(j, 2) == 1, lax.div(j + 1, 2), nz - lax.div(j, 2))
+        return lax.rem(my_y + dy, ny) * nz + lax.rem(my_z + dz, nz)
+
+    def along_y(dy):
+        return lax.rem(my_y + dy, ny) * nz + my_z
+
+    def copy_to(src, dst, send_sem, recv_sem, target):
+        return pltpu.make_async_remote_copy(
+            src_ref=src, dst_ref=dst, send_sem=send_sem, recv_sem=recv_sem,
+            device_id={"seq": target}, device_id_type=pl.DeviceIdType.MESH)
 
     def remote(src, dst, number, target):
-        return pltpu.make_async_remote_copy(
-            src_ref=src, dst_ref=dst, send_sem=sems.at[2 * number],
-            recv_sem=sems.at[2 * number + 1], device_id={"seq": target},
-            device_id_type=pl.DeviceIdType.MESH)
+        return copy_to(src, dst, sems.at[2 * number], sems.at[2 * number + 1], target)
+
+    def wait_for(ref, sem):
+        pltpu.make_async_copy(ref, ref, sem).wait()
 
     def wait_sent(ref, number):
-        pltpu.make_async_copy(ref, ref, sems.at[2 * number]).wait()
+        wait_for(ref, sems.at[2 * number])
 
     def wait_arrived(ref, number):
-        pltpu.make_async_copy(ref, ref, sems.at[2 * number + 1]).wait()
-
+        wait_for(ref, sems.at[2 * number + 1])
+
+    loads = [pltpu.make_async_copy(src, dst, in_sems.at[i]) for i, (src, dst) in enumerate(
+        ((proj_in, proj), (w_out_in, w_out), (d_out_in, d_out)))]
+    for load in loads:
+        load.start()
     barrier = pltpu.get_barrier_semaphore()
 
     @pl.loop(1, n)
     def _(step):
         pl.semaphore_signal(barrier, inc=1, device_id={"seq": other(step)},
                             device_id_type=pl.DeviceIdType.MESH)
+
+    for load in loads:
+        load.wait()
 
     grad_att = dot(d_out[...], w_out[...], ((1,), (0,))).astype(BF16)
     ones = jnp.ones((tokens, HS), BF16)
@@ -83,20 +105,15 @@
         payload = jnp.concatenate(
             [(q_unit * gain[0:1, :]).astype(BF16), (k_unit * gain[1:2, :]).astype(BF16),
              proj[:, first + 2 * HS:first + 3 * HS], grad_att[:, h * HS:(h + 1) * HS], ones], axis=1)
-        row, col = ids_row[h], ids_col[h]
-        same = row == col
+        row = ids_row[h].astype(F32)
+        col = jnp.broadcast_to(row, (tokens, tokens)).T
         t0 = lax.broadcasted_iota(jnp.int32, (tokens, tokens), 0)
         t1 = lax.broadcasted_iota(jnp.int32, (tokens, tokens), 1)
-        rank_row = jnp.sum(jnp.where(same & (t0 < t1), 1.0, 0.0), axis=0, keepdims=True).astype(jnp.int32)
-        rank_col = jnp.sum(jnp.where(same & (t1 < t0), 1.0, 0.0), axis=1, keepdims=True).astype(jnp.int32)
-
-        def place(ids, rank):
-            return jnp.where(rank < MAIN, ids * MAIN + rank, n * MAIN + (rank - MAIN) * n + ids)
-
+        rank = jnp.sum(jnp.where((row == col) & (t0 < t1), 1.0, 0.0), axis=0, keepdims=True)
+        code = jnp.where(rank < MAIN, row * MAIN + rank, n * MAIN + (rank - MAIN) * n + row)
+        codes[h] = code
         chooser = jnp.where(
-            place(row, rank_row) == lax.broadcasted_iota(jnp.int32, (slots, tokens), 0), 1.0, 0.0).astype(BF16)
-        chooser_t[h] = jnp.where(
-            place(col, rank_col) == lax.broadcasted_iota(jnp.int32, (tokens, slots), 1), 1.0, 0.0).astype(BF16)
+            code.astype(jnp.int32) == lax.broadcasted_iota(jnp.int32, (slots, tokens), 0), 1.0, 0.0).astype(BF16)
         rows = dot(chooser, payload, ((1,), (0,)))
         live = rows[:, 4 * HS:]
         packed.append([rows[:, :HS], rows[:, HS:2 * HS],
@@ -132,12 +149,18 @@
         remote(sent.at[target], arrived.at[me], 0, target).start()
 
     for dy in range(1, ny):
-        to_y = (my_y + dy) % ny
-        start = pl.multiple_of(to_y * width, width)
-        remote(d_out.at[:, pl.ds(start, width)], d_cols.at[my_y], 1, to_y * nz + my_z).start()
+        start = pl.multiple_of(lax.rem(my_y + dy, ny) * width, width)
+        remote(d_out.at[:, pl.ds(start, width)], d_cols.at[my_y], 1, along_y(dy)).start()
     own = pl.multiple_of(my_y * width, width)
     d_cols[my_y] = d_out[:, pl.ds(own, width)]
     arrived[me] = sent[me]
+    for h in range(HEADS):
+        code = jnp.broadcast_to(codes[h], (tokens, tokens)).T[:, 0:1].astype(jnp.int32)
+        chooser_t[h] = jnp.where(
+            code == lax.broadcasted_iota(jnp.int32, (tokens, slots), 1), 1.0, 0.0).astype(BF16)
+    wait_arrived(d_cols.at[pl.ds(0, ny - 1)], 1)
+    for y in range(ny):
+        d_cols_t[:, y * tokens:(y + 1) * tokens] = d_cols[y].T
 
     wait_arrived(arrived.at[pl.ds(0, n - 1)], 0)
 
@@ -184,17 +207,17 @@
         target = other(step)
         remote(back1.at[target], home1.at[me], 2, target).start()
 
-    @pl.loop(1, n)
-    def _(step):
-        target = other(step)
-        remote(back2.at[target], home2.at[me], 3, target).start()
-
+    bounds = [1 + (n - 1) * i // 10 for i in range(11)]
+
+    def send_batch(i):
+        @pl.loop(bounds[i], bounds[i + 1])
+        def _(step):
+            target = other(step)
+            remote(back2.at[target], home2.at[me], 3, target).start()
+
+    send_batch(0)
     home1[me] = back1[me]
     home2[me] = back2[me]
-
-    wait_arrived(d_cols.at[pl.ds(0, ny - 1)], 1)
-    for y in range(ny):
-        d_cols_t[:, y * tokens:(y + 1) * tokens] = d_cols[y].T
 
     wait_arrived(home1.at[pl.ds(0, n - 1)], 2)
     rest[...] = home1[:, REST_ROW:REST_ROW + TILE].astype(F32).reshape(n * TILE, HS)
@@ -202,20 +225,44 @@
         rows = slots_of(home1[:, 0:TILE], 0, h).astype(BF16)
         att[:, h * HS:(h + 1) * HS] = dot(chooser_t[h], rows, ((1,), (0,))).astype(BF16)
     for dy in range(1, ny):
-        to_y = (my_y + dy) % ny
-        remote(att, att_all.at[my_y], 4, to_y * nz + my_z).start()
+        remote(att, att_all.at[my_y], 4, along_y(dy)).start()
+    send_batch(1)
     att_all[my_y] = att[...]
     wait_arrived(att_all.at[pl.ds(0, ny - 1)], 4)
     gathered = att_all[...].reshape(ny * tokens, HEADS * HS)
-    rows_z = width // nz
-    part[...] = dot(d_cols_t[...], gathered, ((1,), (0,))).astype(BF16).reshape(nz, rows_z, HEADS * HS)
-
-    @pl.loop(1, nz)
-    def _(step):
-        to_z = (my_z + jnp.where(step % 2 == 1, (step + 1) // 2, nz - step // 2)) % nz
-        remote(part.at[to_z], part_all.at[my_z], 5, my_y * nz + to_z).start()
-
-    part_all[my_z] = part[my_z]
+    part[...] = dot(d_cols_t[...], gathered, ((1,), (0,)))
+
+    half = nz // 2
+    right = my_y * nz + lax.rem(my_z + 1, nz)
+    left = my_y * nz + lax.rem(my_z + nz - 1, nz)
+
+    def part_of(away):
+        start = pl.multiple_of(lax.rem(my_z + away, nz) * rows_z, rows_z)
+        return part[pl.ds(start, rows_z), :]
+
+    def ring_copies(k):
+        copies = [copy_to(out_r.at[k], in_r.at[k], ring_sems.at[0], ring_sems.at[2 + k], right)]
+        if k < half - 1:
+            copies.append(copy_to(out_l.at[k], in_l.at[k], ring_sems.at[1], ring_sems.at[2 + half + k], left))
+        return copies
+
+    for k in range(half):
+        to_right, to_left = part_of(half - k), part_of(nz - half + 1 + k)
+        if k > 0:
+            to_right = to_right + in_r[k - 1].astype(F32)
+            if k < half - 1:
+                to_left = to_left + in_l[k - 1].astype(F32)
+        out_r[k] = to_right.astype(BF16)
+        if k < half - 1:
+            out_l[k] = to_left.astype(BF16)
+        for copy in ring_copies(k):
+            copy.start()
+        for i in range(2 + k * 8 // half, 2 + (k + 1) * 8 // half):
+            send_batch(i)
+        for copy in ring_copies(k):
+            copy.wait_recv()
+    total = part_of(0) + in_r[half - 1].astype(F32) + in_l[half - 2].astype(F32)
+    d_w[...] = total * (tokens * n) ** -0.5
 
     wait_arrived(home2.at[pl.ds(0, n - 1)], 3)
     for h in range(HEADS):
@@ -231,18 +278,13 @@
                 unit, inverse, gain[c:c + 1, :], found[:, c * HS:(c + 1) * HS]).astype(BF16)
         d_proj[:, first + 2 * HS:first + 3 * HS] = found[:, 2 * HS:].astype(BF16)
 
-    wait_arrived(part_all.at[pl.ds(0, nz - 1)], 5)
-    total = part_all[0].astype(F32)
-    for z in range(1, nz):
-        total = total + part_all[z].astype(F32)
-    d_w[...] = total * (tokens * n) ** -0.5
-
     wait_sent(sent.at[pl.ds(0, n - 1)], 0)
     wait_sent(d_cols.at[pl.ds(0, ny - 1)], 1)
     wait_sent(back1.at[pl.ds(0, n - 1)], 2)
     wait_sent(back2.at[pl.ds(0, n - 1)], 3)
     wait_sent(att_all.at[pl.ds(0, ny - 1)], 4)
-    wait_sent(part.at[pl.ds(0, nz - 1)], 5)
+    wait_for(out_r, ring_sems.at[0])
+    wait_for(out_l, ring_sems.at[1])
 
 
 def per_device(ny, projections, qk_gain, clusters, d_out, w_out):
@@ -253,30 +295,39 @@
     width = d_out.shape[1] // ny
     columns = HEADS * HS
     vmem = pltpu.VMEM
+    half = nz // 2
+    ring = (width // nz, columns)
     scratch = [
+        vmem(projections.shape, BF16), vmem(d_out.shape, BF16), vmem(w_out.shape, BF16),
         vmem((n, ROWS, HS), BF16), vmem((n, ROWS, HS), BF16),
         vmem((n, FIRST, HS), BF16), vmem((n, ROWS - FIRST, HS), BF16),
         vmem((n, FIRST, HS), BF16), vmem((n, ROWS - FIRST, HS), BF16),
         vmem((n * TILE, HS), F32),
         vmem((ny, tokens, width), BF16), vmem((width, ny * tokens), BF16),
         vmem((tokens, columns), BF16), vmem((ny, tokens, columns), BF16),
-        vmem((nz, width // nz, columns), BF16), vmem((nz, width // nz, columns), BF16),
+        vmem((width, columns), F32),
+        vmem((half, *ring), BF16), vmem((half - 1, *ring), BF16),
+        vmem((half, *ring), BF16), vmem((half - 1, *ring), BF16),
         vmem((slots, HS), BF16), vmem((slots, HS), BF16), vmem((slots, HS), BF16), vmem((slots, HS), BF16),
         vmem((slots, slots), BF16), vmem((slots, slots), BF16),
-        vmem((HEADS, tokens, slots), BF16),
-        pltpu.SemaphoreType.DMA((12,)),
+        vmem((HEADS, 1, tokens), F32), vmem((HEADS, tokens, slots), BF16),
+        pltpu.SemaphoreType.DMA((3,)), pltpu.SemaphoreType.DMA((10,)), pltpu.SemaphoreType.DMA((2 + nz - 1,)),
     ]
     whole = pl.BlockSpec(memory_space=pltpu.VMEM)
-    return pl.pallas_call(
+    anywhere = pl.BlockSpec(memory_space=pl.ANY)
+    shapes = (jax.ShapeDtypeStruct(projections.shape, BF16),
+              jax.ShapeDtypeStruct((width // nz, columns), F32))
+    results = pl.pallas_call(
         functools.partial(kernel, ny, nz),
-        out_shape=(jax.ShapeDtypeStruct(projections.shape, BF16),
-                   jax.ShapeDtypeStruct((width // nz, columns), F32)),
-        in_specs=[whole] * 6,
+        out_shape=shapes,
+        in_specs=[whole] * 2 + [anywhere] * 3,
         out_specs=(whole, whole),
         scratch_shapes=scratch,
         compiler_params=pltpu.CompilerParams(
             collective_id=0, has_side_effects=True, vmem_limit_bytes=56 * 1024 * 1024),
-    )(projections, qk_gain, clusters.reshape(HEADS, 1, tokens), clusters, d_out, w_out)
+    )(qk_gain, clusters.reshape(HEADS, 1, tokens), projections, d_out, w_out)
+    return pl.pallas_call(
+        write_out, out_shape=shapes, in_specs=[whole] * 2, out_specs=(whole, whole))(*results)
 
 
 def solution(mesh):

time: 172 us -> 162 us (0.942)
  the two profiles are of different devices: /device:TPU:40 before, /device:TPU:4 now
where the time goes in v2:
time: 162 us; the launch traced here: 161 us
  Pallas kernels  161 us (99%)
    pallas_call x1, Pallas kernels, per_device(): pl.pallas_call(functools.partial(kernel, ny, nz), out_shape=shapes, in_sp...  159 us

profile of v2, /device:TPU:4, one launch (start us, length us, event | category | flops | bytes accessed | tf_op | source)
XLA Modules:
  0.0 161.4 jit_solution(10682867559320595615)
XLA Ops:
  0.6 159.0 %shard_map.68 = (bf16[256,768]{1,0:T(8,128)(2,1)}, f32[64,256]{1,0:T(8,128)}) custom-call(f32[2,128]{1,0:T(2,128)} %gain.1, s32[2,1,256]{2,1,0:T(1,128)} %bitcast.1, bf16[256,768]{1,0:T(8,128)(2,1)} %proj_in.1, bf16[256,4096]{1,0:T(8,128)(2,1)} %d_out_in.1, bf16[4096,256]{1,0:T(8,128)(2,1)} %w_out_in.1), custom_call_target="tpu_custom_call" | custom-call | tf_op jit(solution)/shard_map/pallas_call | solution.py:320
  159.6 1.8 %shard_map.69 = (bf16[256,768]{1,0:T(8,128)(2,1)}, f32[64,256]{1,0:T(8,128)}) custom-call(bf16[256,768]{1,0:T(8,128)(2,1)} %get-tuple-element.4.d_proj, f32[64,256]{1,0:T(8,128)} %get-tuple-element.5.d_w), custom_call_target="tpu_custom_call" | custom-call | tf_op jit(solution)/shard_map/pallas_call | solution.py:329

commit v3 on v2

--- a/solution.py
+++ b/solution.py
@@ -20,7 +20,9 @@
 MAIN_ROW = (0, 32, 48, 64)
 REST_ROW = 16
 ROWS = 80
-FIRST = 32
+HALF = TILE // 2
+FIRST = TILE + HALF
+WEIGHTS = (0.12, 0.35)
 
 
 def dot(a, b, dims):
@@ -43,8 +45,22 @@
     d_w_out[...] = d_w[...]
 
 
+def batch_bounds(ny, nz, parts):
+    n = ny * nz
+    hops = [((n - step) // ny + 1) // 2 for step in range(1, n)]
+    whole, bounds, done, share = sum(hops), [1], 0, 0.0
+    for part in parts[:-1]:
+        share += part
+        step = bounds[-1]
+        while step < n and done + hops[step - 1] / 2 <= share * whole:
+            done += hops[step - 1]
+            step += 1
+        bounds.append(step)
+    return bounds + [n]
+
+
 def kernel(ny, nz, gain, ids_row, proj_in, d_out_in, w_out_in, d_proj, d_w,
-           proj, d_out, w_out, sent, arrived, back1, back2, home1, home2, rest, d_cols, d_cols_t,
+           proj, d_out, w_out, sent, arrived, back1, back2, home1, home2, rest, rest1, rest2, d_cols, d_cols_t,
            att, att_all, part, out_r, out_l, in_r, in_l, qs, ks, vs, gs, low, grad_low,
            codes, chooser_t, in_sems, sems, ring_sems):
     n = ny * nz
@@ -55,10 +71,12 @@
     me = lax.axis_index("seq")
     my_y, my_z = lax.div(me, nz), lax.rem(me, nz)
 
-    def other(step):
+    def other(step, mirror=False):
         step = n - step
         j, dy = lax.div(step, ny), lax.rem(step, ny)
         dz = jnp.where(lax.rem(j, 2) == 1, lax.div(j + 1, 2), nz - lax.div(j, 2))
+        if mirror:
+            dz = jnp.where(2 * dy < ny, dz, 2 * nz - dz)
         return lax.rem(my_y + dy, ny) * nz + lax.rem(my_z + dz, nz)
 
     def along_y(dy):
@@ -123,7 +141,7 @@
         both = [parts[h][c][:n * MAIN].reshape(n, MAIN, HS) for h in range(HEADS)]
         return jnp.concatenate(both, axis=1).astype(BF16)
 
-    def rest_tile(parts):
+    def fill_rest(parts):
         for h in range(HEADS):
             for c in range(4):
                 for r in range(CAP - MAIN):
@@ -131,15 +149,15 @@
                     rest[pl.ds(c * 4 + h * 2 + r, n, stride=TILE), :] = parts[h][c][start:start + n]
         return rest[...].reshape(n, TILE, HS).astype(BF16)
 
-    def slots_of(main, c, h):
+    def slots_of(main, c, h, rest=rest, stride=TILE):
         pieces = [main.astype(F32)[:, h * MAIN:(h + 1) * MAIN].reshape(n * MAIN, HS)]
         for r in range(CAP - MAIN):
-            pieces.append(rest[pl.ds(c * 4 + h * 2 + r, n, stride=TILE), :])
+            pieces.append(rest[pl.ds(c * 4 + h * 2 + r, n, stride=stride), :])
         return jnp.concatenate(pieces, axis=0)
 
     for c in range(4):
         sent[:, MAIN_ROW[c]:MAIN_ROW[c] + TILE] = main_tile(packed, c)
-    sent[:, REST_ROW:REST_ROW + TILE] = rest_tile(packed)
+    sent[:, REST_ROW:REST_ROW + TILE] = fill_rest(packed)
 
     pl.semaphore_wait(barrier, n - 1)
 
@@ -196,23 +214,24 @@
         grad_k = dot(grad_low[...], qs[...], ((1,), (0,)))
         grad_v = dot(low[...], gs[...], ((1,), (0,)))
         results.append([out, grad_q, grad_k, grad_v])
-    back1[:, REST_ROW:REST_ROW + TILE] = rest_tile(results)
+    back_rest = fill_rest(results)
     back1[:, 0:TILE] = main_tile(results, 0)
+    back1[:, TILE:] = back_rest[:, :HALF]
     for c in range(1, 4):
-        start = MAIN_ROW[c] - FIRST
-        back2[:, start:start + TILE] = main_tile(results, c)
+        back2[:, (c - 1) * TILE:c * TILE] = main_tile(results, c)
+    back2[:, 3 * TILE:] = back_rest[:, HALF:]
 
     @pl.loop(1, n)
     def _(step):
         target = other(step)
         remote(back1.at[target], home1.at[me], 2, target).start()
 
-    bounds = [1 + (n - 1) * i // 10 for i in range(11)]
+    bounds = batch_bounds(ny, nz, WEIGHTS + ((1 - sum(WEIGHTS)) / (nz // 2),) * (nz // 2))
 
     def send_batch(i):
         @pl.loop(bounds[i], bounds[i + 1])
         def _(step):
-            target = other(step)
+            target = other(step, mirror=True)
             remote(back2.at[target], home2.at[me], 3, target).start()
 
     send_batch(0)
@@ -220,9 +239,9 @@
     home2[me] = back2[me]
 
     wait_arrived(home1.at[pl.ds(0, n - 1)], 2)
-    rest[...] = home1[:, REST_ROW:REST_ROW + TILE].astype(F32).reshape(n * TILE, HS)
-    for h in range(HEADS):
-        rows = slots_of(home1[:, 0:TILE], 0, h).astype(BF16)
+    rest1[...] = home1[:, TILE:].astype(F32).reshape(n * HALF, HS)
+    for h in range(HEADS):
+        rows = slots_of(home1[:, 0:TILE], 0, h, rest1, HALF).astype(BF16)
         att[:, h * HS:(h + 1) * HS] = dot(chooser_t[h], rows, ((1,), (0,))).astype(BF16)
     for dy in range(1, ny):
         remote(att, att_all.at[my_y], 4, along_y(dy)).start()
@@ -257,19 +276,20 @@
             out_l[k] = to_left.astype(BF16)
         for copy in ring_copies(k):
             copy.start()
-        for i in range(2 + k * 8 // half, 2 + (k + 1) * 8 // half):
-            send_batch(i)
+        send_batch(len(WEIGHTS) + k)
         for copy in ring_copies(k):
             copy.wait_recv()
     total = part_of(0) + in_r[half - 1].astype(F32) + in_l[half - 2].astype(F32)
     d_w[...] = total * (tokens * n) ** -0.5
 
     wait_arrived(home2.at[pl.ds(0, n - 1)], 3)
+    rest2[...] = home2[:, 3 * TILE:].astype(F32).reshape(n * HALF, HS)
     for h in range(HEADS):
         grads = []
         for c in range(1, 4):
-            start = MAIN_ROW[c] - FIRST
-            grads.append(slots_of(home2[:, start:start + TILE], c, h).astype(BF16))
+            main = home2[:, (c - 1) * TILE:c * TILE]
+            spare = rest1 if c == 1 else rest2
+            grads.append(slots_of(main, c if c == 1 else c - 2, h, spare, HALF).astype(BF16))
         found = dot(chooser_t[h], jnp.concatenate(grads, axis=1), ((1,), (0,)))
         first = h * 3 * HS
         for c in range(2):
@@ -302,7 +322,7 @@
         vmem((n, ROWS, HS), BF16), vmem((n, ROWS, HS), BF16),
         vmem((n, FIRST, HS), BF16), vmem((n, ROWS - FIRST, HS), BF16),
         vmem((n, FIRST, HS), BF16), vmem((n, ROWS - FIRST, HS), BF16),
-        vmem((n * TILE, HS), F32),
+        vmem((n * TILE, HS), F32), vmem((n * HALF, HS), F32), vmem((n * HALF, HS), F32),
         vmem((ny, tokens, width), BF16), vmem((width, ny * tokens), BF16),
         vmem((tokens, columns), BF16), vmem((ny, tokens, columns), BF16),
         vmem((width, columns), F32),

time: 162 us -> 157 us (0.969)
  Pallas kernels: 161 us -> 157 us
    pallas_call x1, Pallas kernels: 159 us -> 155 us  [per_device(): pl.pallas_call(functools.partial(kernel, ny, nz), out_shape=shapes, in_sp...]
where the time goes in v3:
time: 157 us
  Pallas kernels  157 us (100%)
    pallas_call x1, Pallas kernels, per_device(): pl.pallas_call(functools.partial(kernel, ny, nz), out_shape=shapes, in_sp...  155 us

profile of v3, /device:TPU:4, one launch (start us, length us, event | category | flops | bytes accessed | tf_op | source)
XLA Modules:
  0.0 157.3 jit_solution(9778710397449069899)
XLA Ops:
  0.6 154.9 %shard_map.68 = (bf16[256,768]{1,0:T(8,128)(2,1)}, f32[64,256]{1,0:T(8,128)}) custom-call(f32[2,128]{1,0:T(2,128)} %gain.1, s32[2,1,256]{2,1,0:T(1,128)} %bitcast.1, bf16[256,768]{1,0:T(8,128)(2,1)} %proj_in.1, bf16[256,4096]{1,0:T(8,128)(2,1)} %d_out_in.1, bf16[4096,256]{1,0:T(8,128)(2,1)} %w_out_in.1), custom_call_target="tpu_custom_call" | custom-call | tf_op jit(solution)/shard_map/pallas_call | solution.py:340
  155.5 1.8 %shard_map.69 = (bf16[256,768]{1,0:T(8,128)(2,1)}, f32[64,256]{1,0:T(8,128)}) custom-call(bf16[256,768]{1,0:T(8,128)(2,1)} %get-tuple-element.4.d_proj, f32[64,256]{1,0:T(8,128)} %get-tuple-element.5.d_w), custom_call_target="tpu_custom_call" | custom-call | tf_op jit(solution)/shard_map/pallas_call | solution.py:349

commit v4 on v3

--- a/solution.py
+++ b/solution.py
@@ -13,16 +13,14 @@
 CAP = 10
 MAIN = 8
 DEAD = 1024.0
-TILE = 16
 F32 = jnp.float32
 BF16 = jnp.bfloat16
 
-MAIN_ROW = (0, 32, 48, 64)
-REST_ROW = 16
-ROWS = 80
-HALF = TILE // 2
-FIRST = TILE + HALF
-WEIGHTS = (0.12, 0.35)
+BLOCK = 8
+OUT_BLOCKS = 5
+BACK = (((0, 2),), ((0, 0), (1, 0)), ((0, 1), (1, 1), (1, 2), (0, 3), (1, 3)))
+REST = (False, True, True)
+WEIGHTS = (0.15, 0.35, 0.15)
 
 
 def dot(a, b, dims):
@@ -60,8 +58,9 @@
 
 
 def kernel(ny, nz, gain, ids_row, proj_in, d_out_in, w_out_in, d_proj, d_w,
-           proj, d_out, w_out, sent, arrived, back1, back2, home1, home2, rest, rest1, rest2, d_cols, d_cols_t,
-           att, att_all, part, out_r, out_l, in_r, in_l, qs, ks, vs, gs, low, grad_low,
+           proj, d_out, w_out, sent, arrived, back0, back1, back2, home0, home1, home2,
+           rest, rest_a, rest_b, d_cols, d_cols_t, att, att_all, part, mine, pair_out, pair_in,
+           out_r, out_l, in_r, in_l, qs, ks, vs, gs, low, grad_low,
            codes, chooser_t, in_sems, sems, ring_sems):
     n = ny * nz
     tokens = proj.shape[0]
@@ -115,8 +114,34 @@
 
     grad_att = dot(d_out[...], w_out[...], ((1,), (0,))).astype(BF16)
     ones = jnp.ones((tokens, HS), BF16)
-    packed = []
-    for h in range(HEADS):
+
+    def main_block(rows):
+        return rows[:n * MAIN].reshape(n, MAIN, HS)
+
+    def put_rest(ref, at, rows):
+        for r in range(CAP - MAIN):
+            start = n * (MAIN + r)
+            ref[pl.ds(at + r, n, stride=BLOCK), :] = rows[start:start + n]
+
+    def rest_block(ref):
+        return ref[...].reshape(n, BLOCK, HS)
+
+    def slots_of(block, ref, at):
+        pieces = [block.reshape(n * MAIN, HS)]
+        for r in range(CAP - MAIN):
+            pieces.append(ref[pl.ds(at + r, n, stride=BLOCK), :])
+        return jnp.concatenate(pieces, axis=0)
+
+    def block_of(message, i):
+        return message[:, i * BLOCK:(i + 1) * BLOCK]
+
+    def to_all(src, dst, number, steps=(1, n), mirror=False):
+        @pl.loop(*steps)
+        def _(step):
+            target = other(step, mirror)
+            remote(src.at[target], dst.at[me], number, target).start()
+
+    def pack(h):
         first = h * 3 * HS
         q_unit, _ = normalize(proj[:, first:first + HS])
         k_unit, _ = normalize(proj[:, first + HS:first + 2 * HS])
@@ -134,60 +159,36 @@
             code.astype(jnp.int32) == lax.broadcasted_iota(jnp.int32, (slots, tokens), 0), 1.0, 0.0).astype(BF16)
         rows = dot(chooser, payload, ((1,), (0,)))
         live = rows[:, 4 * HS:]
-        packed.append([rows[:, :HS], rows[:, HS:2 * HS],
-                       rows[:, 2 * HS:3 * HS] + (1.0 - live) * DEAD, rows[:, 3 * HS:4 * HS]])
-
-    def main_tile(parts, c):
-        both = [parts[h][c][:n * MAIN].reshape(n, MAIN, HS) for h in range(HEADS)]
-        return jnp.concatenate(both, axis=1).astype(BF16)
-
-    def fill_rest(parts):
-        for h in range(HEADS):
-            for c in range(4):
-                for r in range(CAP - MAIN):
-                    start = n * (MAIN + r)
-                    rest[pl.ds(c * 4 + h * 2 + r, n, stride=TILE), :] = parts[h][c][start:start + n]
-        return rest[...].reshape(n, TILE, HS).astype(BF16)
-
-    def slots_of(main, c, h, rest=rest, stride=TILE):
-        pieces = [main.astype(F32)[:, h * MAIN:(h + 1) * MAIN].reshape(n * MAIN, HS)]
-        for r in range(CAP - MAIN):
-            pieces.append(rest[pl.ds(c * 4 + h * 2 + r, n, stride=stride), :])
-        return jnp.concatenate(pieces, axis=0)
-
-    for c in range(4):
-        sent[:, MAIN_ROW[c]:MAIN_ROW[c] + TILE] = main_tile(packed, c)
-    sent[:, REST_ROW:REST_ROW + TILE] = fill_rest(packed)
-
+        parts = [rows[:, :HS], rows[:, HS:2 * HS],
+                 rows[:, 2 * HS:3 * HS] + (1.0 - live) * DEAD, rows[:, 3 * HS:4 * HS]]
+        for c in range(4):
+            put_rest(rest, c * 2, parts[c])
+        sent[h] = jnp.concatenate([main_block(p) for p in parts] + [rest_block(rest)], axis=1).astype(BF16)
+
+    pack(0)
     pl.semaphore_wait(barrier, n - 1)
-
-    @pl.loop(1, n)
-    def _(step):
-        target = other(step)
-        remote(sent.at[target], arrived.at[me], 0, target).start()
+    to_all(sent.at[0], arrived.at[0], 0)
+    pack(1)
+    to_all(sent.at[1], arrived.at[1], 1)
 
     for dy in range(1, ny):
         start = pl.multiple_of(lax.rem(my_y + dy, ny) * width, width)
-        remote(d_out.at[:, pl.ds(start, width)], d_cols.at[my_y], 1, along_y(dy)).start()
+        remote(d_out.at[:, pl.ds(start, width)], d_cols.at[my_y], 2, along_y(dy)).start()
     own = pl.multiple_of(my_y * width, width)
     d_cols[my_y] = d_out[:, pl.ds(own, width)]
-    arrived[me] = sent[me]
-    for h in range(HEADS):
+    for h in range(HEADS):
+        arrived[h, me] = sent[h, me]
         code = jnp.broadcast_to(codes[h], (tokens, tokens)).T[:, 0:1].astype(jnp.int32)
         chooser_t[h] = jnp.where(
             code == lax.broadcasted_iota(jnp.int32, (tokens, slots), 1), 1.0, 0.0).astype(BF16)
-    wait_arrived(d_cols.at[pl.ds(0, ny - 1)], 1)
-    for y in range(ny):
-        d_cols_t[:, y * tokens:(y + 1) * tokens] = d_cols[y].T
-
-    wait_arrived(arrived.at[pl.ds(0, n - 1)], 0)
-
-    rest[...] = arrived[:, REST_ROW:REST_ROW + TILE].astype(F32).reshape(n * TILE, HS)
+
     scale = HS ** -0.5
-    results = []
-    for h in range(HEADS):
+
+    def own_cluster(h):
+        message = arrived[h].astype(F32)
+        rest[...] = block_of(message, OUT_BLOCKS - 1).reshape(n * BLOCK, HS)
         for c, ref in enumerate((qs, ks, vs, gs)):
-            rows = slots_of(arrived[:, MAIN_ROW[c]:MAIN_ROW[c] + TILE], c, h)
+            rows = slots_of(block_of(message, c), rest, c * 2)
             if c == 2:
                 live = jnp.where(rows < DEAD / 2, 1.0, 0.0)[:, 0:1]
                 rows = jnp.where(rows < DEAD / 2, rows, 0.0)
@@ -213,51 +214,73 @@
         grad_q = jnp.concatenate(grad_q_t, axis=1).T
         grad_k = dot(grad_low[...], qs[...], ((1,), (0,)))
         grad_v = dot(low[...], gs[...], ((1,), (0,)))
-        results.append([out, grad_q, grad_k, grad_v])
-    back_rest = fill_rest(results)
-    back1[:, 0:TILE] = main_tile(results, 0)
-    back1[:, TILE:] = back_rest[:, :HALF]
-    for c in range(1, 4):
-        back2[:, (c - 1) * TILE:c * TILE] = main_tile(results, c)
-    back2[:, 3 * TILE:] = back_rest[:, HALF:]
-
-    @pl.loop(1, n)
-    def _(step):
-        target = other(step)
-        remote(back1.at[target], home1.at[me], 2, target).start()
-
-    bounds = batch_bounds(ny, nz, WEIGHTS + ((1 - sum(WEIGHTS)) / (nz // 2),) * (nz // 2))
+        parts = [out, grad_q, grad_k, grad_v]
+        for c in range(4):
+            put_rest(rest_a if c < 2 else rest_b, c % 2 * 4 + h * 2, parts[c])
+        return [main_block(p) for p in parts]
+
+    def message_back(i, results):
+        blocks = [results[h][c] for h, c in BACK[i]]
+        if REST[i]:
+            blocks.append(rest_block(rest_a if i == 1 else rest_b))
+        return jnp.concatenate(blocks, axis=1).astype(BF16)
+
+    wait_arrived(arrived.at[0, pl.ds(0, n - 1)], 0)
+    results = [own_cluster(0)]
+    back0[...] = message_back(0, results)
+    to_all(back0, home0, 3)
+    home0[me] = back0[me]
+    wait_arrived(d_cols.at[pl.ds(0, ny - 1)], 2)
+    for y in range(ny):
+        d_cols_t[:, y * tokens:(y + 1) * tokens] = d_cols[y].T
+    wait_arrived(arrived.at[1, pl.ds(0, n - 1)], 1)
+    results.append(own_cluster(1))
+    back1[...] = message_back(1, results)
+    to_all(back1, home1, 4)
+    back2[...] = message_back(2, results)
+
+    members = nz // 2
+    half = members // 2
+    bounds = batch_bounds(ny, nz, WEIGHTS + ((1 - sum(WEIGHTS)) / half,) * half)
 
     def send_batch(i):
-        @pl.loop(bounds[i], bounds[i + 1])
-        def _(step):
-            target = other(step, mirror=True)
-            remote(back2.at[target], home2.at[me], 3, target).start()
+        to_all(back2, home2, 5, (bounds[i], bounds[i + 1]), mirror=True)
 
     send_batch(0)
     home1[me] = back1[me]
     home2[me] = back2[me]
 
-    wait_arrived(home1.at[pl.ds(0, n - 1)], 2)
-    rest1[...] = home1[:, TILE:].astype(F32).reshape(n * HALF, HS)
-    for h in range(HEADS):
-        rows = slots_of(home1[:, 0:TILE], 0, h, rest1, HALF).astype(BF16)
+    wait_arrived(home1.at[pl.ds(0, n - 1)], 4)
+    message = home1[...].astype(F32)
+    rest_a[...] = block_of(message, len(BACK[1])).reshape(n * BLOCK, HS)
+    for h in range(HEADS):
+        rows = slots_of(block_of(message, h), rest_a, h * 2).astype(BF16)
         att[:, h * HS:(h + 1) * HS] = dot(chooser_t[h], rows, ((1,), (0,))).astype(BF16)
     for dy in range(1, ny):
-        remote(att, att_all.at[my_y], 4, along_y(dy)).start()
+        remote(att, att_all.at[my_y], 6, along_y(dy)).start()
     send_batch(1)
     att_all[my_y] = att[...]
-    wait_arrived(att_all.at[pl.ds(0, ny - 1)], 4)
+    wait_arrived(att_all.at[pl.ds(0, ny - 1)], 6)
     gathered = att_all[...].reshape(ny * tokens, HEADS * HS)
-    part[...] = dot(d_cols_t[...], gathered, ((1,), (0,)))
-
-    half = nz // 2
-    right = my_y * nz + lax.rem(my_z + 1, nz)
-    left = my_y * nz + lax.rem(my_z + nz - 1, nz)
+    part[...] = dot(d_cols_t[...], gathered, ((1,), (0,))).reshape(members, 2, rows_z, HEADS * HS)
+
+    odd = lax.rem(my_z, 2)
+    for h in range(HEADS):
+        side = 1 - 2 * odd if h == 0 else 2 * odd - 1
+        partner = my_y * nz + lax.rem(my_z + side + nz, nz)
+        pair_out[h] = part[:, 1 - odd, :, h * HS:(h + 1) * HS].astype(BF16)
+        remote(pair_out.at[h], pair_in.at[h], 7 + h, partner).start()
+    send_batch(2)
+    for h in range(HEADS):
+        wait_arrived(pair_in.at[h], 7 + h)
+        mine[:, :, h * HS:(h + 1) * HS] = part[:, odd, :, h * HS:(h + 1) * HS] + pair_in[h].astype(F32)
+
+    my_place = lax.div(my_z, 2)
+    right = my_y * nz + lax.rem(my_z + 2, nz)
+    left = my_y * nz + lax.rem(my_z + nz - 2, nz)
 
     def part_of(away):
-        start = pl.multiple_of(lax.rem(my_z + away, nz) * rows_z, rows_z)
-        return part[pl.ds(start, rows_z), :]
+        return mine[lax.rem(my_place + away, members)]
 
     def ring_copies(k):
         copies = [copy_to(out_r.at[k], in_r.at[k], ring_sems.at[0], ring_sems.at[2 + k], right)]
@@ -266,7 +289,7 @@
         return copies
 
     for k in range(half):
-        to_right, to_left = part_of(half - k), part_of(nz - half + 1 + k)
+        to_right, to_left = part_of(half - k), part_of(members - half + 1 + k)
         if k > 0:
             to_right = to_right + in_r[k - 1].astype(F32)
             if k < half - 1:
@@ -282,14 +305,15 @@
     total = part_of(0) + in_r[half - 1].astype(F32) + in_l[half - 2].astype(F32)
     d_w[...] = total * (tokens * n) ** -0.5
 
-    wait_arrived(home2.at[pl.ds(0, n - 1)], 3)
-    rest2[...] = home2[:, 3 * TILE:].astype(F32).reshape(n * HALF, HS)
+    wait_arrived(home0.at[pl.ds(0, n - 1)], 3)
+    wait_arrived(home2.at[pl.ds(0, n - 1)], 5)
+    first_message, message = home0[...].astype(F32), home2[...].astype(F32)
+    rest_b[...] = block_of(message, len(BACK[2])).reshape(n * BLOCK, HS)
     for h in range(HEADS):
         grads = []
         for c in range(1, 4):
-            main = home2[:, (c - 1) * TILE:c * TILE]
-            spare = rest1 if c == 1 else rest2
-            grads.append(slots_of(main, c if c == 1 else c - 2, h, spare, HALF).astype(BF16))
+            block = first_message if (h, c) in BACK[0] else block_of(message, BACK[2].index((h, c)))
+            grads.append(slots_of(block, rest_a if c < 2 else rest_b, c % 2 * 4 + h * 2).astype(BF16))
         found = dot(chooser_t[h], jnp.concatenate(grads, axis=1), ((1,), (0,)))
         first = h * 3 * HS
         for c in range(2):
@@ -298,11 +322,15 @@
                 unit, inverse, gain[c:c + 1, :], found[:, c * HS:(c + 1) * HS]).astype(BF16)
         d_proj[:, first + 2 * HS:first + 3 * HS] = found[:, 2 * HS:].astype(BF16)
 
-    wait_sent(sent.at[pl.ds(0, n - 1)], 0)
-    wait_sent(d_cols.at[pl.ds(0, ny - 1)], 1)
-    wait_sent(back1.at[pl.ds(0, n - 1)], 2)
-    wait_sent(back2.at[pl.ds(0, n - 1)], 3)
-    wait_sent(att_all.at[pl.ds(0, ny - 1)], 4)
+    for h in range(HEADS):
+        wait_sent(sent.at[h, pl.ds(0, n - 1)], h)
+    wait_sent(d_cols.at[pl.ds(0, ny - 1)], 2)
+    wait_sent(back0.at[pl.ds(0, n - 1)], 3)
+    wait_sent(back1.at[pl.ds(0, n - 1)], 4)
+    wait_sent(back2.at[pl.ds(0, n - 1)], 5)
+    wait_sent(att_all.at[pl.ds(0, ny - 1)], 6)
+    for h in range(HEADS):
+        wait_sent(pair_out.at[h], 7 + h)
     wait_for(out_r, ring_sems.at[0])
     wait_for(out_l, ring_sems.at[1])
 
@@ -315,23 +343,26 @@
     width = d_out.shape[1] // ny
     columns = HEADS * HS
     vmem = pltpu.VMEM
-    half = nz // 2
-    ring = (width // nz, columns)
+    members = nz // 2
+    half = members // 2
+    rows_z = width // nz
+    ring = (rows_z, columns)
+    back = [vmem((n, (len(BACK[i]) + REST[i]) * BLOCK, HS), BF16) for i in range(3)]
+    rest = vmem((n * BLOCK, HS), F32)
     scratch = [
         vmem(projections.shape, BF16), vmem(d_out.shape, BF16), vmem(w_out.shape, BF16),
-        vmem((n, ROWS, HS), BF16), vmem((n, ROWS, HS), BF16),
-        vmem((n, FIRST, HS), BF16), vmem((n, ROWS - FIRST, HS), BF16),
-        vmem((n, FIRST, HS), BF16), vmem((n, ROWS - FIRST, HS), BF16),
-        vmem((n * TILE, HS), F32), vmem((n * HALF, HS), F32), vmem((n * HALF, HS), F32),
+        vmem((HEADS, n, OUT_BLOCKS * BLOCK, HS), BF16), vmem((HEADS, n, OUT_BLOCKS * BLOCK, HS), BF16),
+        *back, *back, rest, rest, rest,
         vmem((ny, tokens, width), BF16), vmem((width, ny * tokens), BF16),
         vmem((tokens, columns), BF16), vmem((ny, tokens, columns), BF16),
-        vmem((width, columns), F32),
+        vmem((members, 2, *ring), F32), vmem((members, *ring), F32),
+        vmem((HEADS, members, rows_z, HS), BF16), vmem((HEADS, members, rows_z, HS), BF16),
         vmem((half, *ring), BF16), vmem((half - 1, *ring), BF16),
         vmem((half, *ring), BF16), vmem((half - 1, *ring), BF16),
         vmem((slots, HS), BF16), vmem((slots, HS), BF16), vmem((slots, HS), BF16), vmem((slots, HS), BF16),
         vmem((slots, slots), BF16), vmem((slots, slots), BF16),
         vmem((HEADS, 1, tokens), F32), vmem((HEADS, tokens, slots), BF16),
-        pltpu.SemaphoreType.DMA((3,)), pltpu.SemaphoreType.DMA((10,)), pltpu.SemaphoreType.DMA((2 + nz - 1,)),
+        pltpu.SemaphoreType.DMA((3,)), pltpu.SemaphoreType.DMA((18,)), pltpu.SemaphoreType.DMA((2 + members - 1,)),
     ]
     whole = pl.BlockSpec(memory_space=pltpu.VMEM)
     anywhere = pl.BlockSpec(memory_space=pl.ANY)

time: 157 us -> 149 us (0.949)
  the two profiles are of different devices: /device:TPU:4 before, /device:TPU:1 now
where the time goes in v4:
time: 149 us
  Pallas kernels  148 us (99%)
    pallas_call x1, Pallas kernels, per_device(): pl.pallas_call(functools.partial(kernel, ny, nz), out_shape=shapes, in_sp...  146 us

profile of v4, /device:TPU:1, one launch (start us, length us, event | category | flops | bytes accessed | tf_op | source)
XLA Modules:
  0.0 148.5 jit_solution(3032800877275529103)
XLA Ops:
  0.6 146.1 %shard_map.68 = (bf16[256,768]{1,0:T(8,128)(2,1)}, f32[64,256]{1,0:T(8,128)}) custom-call(f32[2,128]{1,0:T(2,128)} %gain.1, s32[2,1,256]{2,1,0:T(1,128)} %bitcast.1, bf16[256,768]{1,0:T(8,128)(2,1)} %proj_in.1, bf16[256,4096]{1,0:T(8,128)(2,1)} %d_out_in.1, bf16[4096,256]{1,0:T(8,128)(2,1)} %w_out_in.1), custom_call_target="tpu_custom_call" | custom-call | tf_op jit(solution)/shard_map/pallas_call | solution.py:371
  146.7 1.8 %shard_map.69 = (bf16[256,768]{1,0:T(8,128)(2,1)}, f32[64,256]{1,0:T(8,128)}) custom-call(bf16[256,768]{1,0:T(8,128)(2,1)} %get-tuple-element.4.d_proj, f32[64,256]{1,0:T(8,128)} %get-tuple-element.5.d_w), custom_call_target="tpu_custom_call" | custom-call | tf_op jit(solution)/shard_map/pallas_call | solution.py:380

commit v5 on v4

--- a/solution.py
+++ b/solution.py
@@ -18,7 +18,7 @@
 
 BLOCK = 8
 OUT_BLOCKS = 5
-BACK = (((0, 2),), ((0, 0), (1, 0)), ((0, 1), (1, 1), (1, 2), (0, 3), (1, 3)))
+BACK = (((0, 0),), ((1, 0),), ((0, 1), (1, 1), (0, 2), (1, 2), (0, 3), (1, 3)))
 REST = (False, True, True)
 WEIGHTS = (0.15, 0.35, 0.15)
 
@@ -251,10 +251,12 @@
     home2[me] = back2[me]
 
     wait_arrived(home1.at[pl.ds(0, n - 1)], 4)
-    message = home1[...].astype(F32)
-    rest_a[...] = block_of(message, len(BACK[1])).reshape(n * BLOCK, HS)
-    for h in range(HEADS):
-        rows = slots_of(block_of(message, h), rest_a, h * 2).astype(BF16)
+    wait_arrived(home0.at[pl.ds(0, n - 1)], 3)
+    first_message, message = home0[...].astype(F32), home1[...].astype(F32)
+    rest_a[...] = block_of(message, 1).reshape(n * BLOCK, HS)
+    for h in range(HEADS):
+        block = block_of((first_message, message)[h], 0)
+        rows = slots_of(block, rest_a, h * 2).astype(BF16)
         att[:, h * HS:(h + 1) * HS] = dot(chooser_t[h], rows, ((1,), (0,))).astype(BF16)
     for dy in range(1, ny):
         remote(att, att_all.at[my_y], 6, along_y(dy)).start()
@@ -305,14 +307,13 @@
     total = part_of(0) + in_r[half - 1].astype(F32) + in_l[half - 2].astype(F32)
     d_w[...] = total * (tokens * n) ** -0.5
 
-    wait_arrived(home0.at[pl.ds(0, n - 1)], 3)
     wait_arrived(home2.at[pl.ds(0, n - 1)], 5)
-    first_message, message = home0[...].astype(F32), home2[...].astype(F32)
+    message = home2[...].astype(F32)
     rest_b[...] = block_of(message, len(BACK[2])).reshape(n * BLOCK, HS)
     for h in range(HEADS):
         grads = []
         for c in range(1, 4):
-            block = first_message if (h, c) in BACK[0] else block_of(message, BACK[2].index((h, c)))
+            block = block_of(message, BACK[2].index((h, c)))
             grads.append(slots_of(block, rest_a if c < 2 else rest_b, c % 2 * 4 + h * 2).astype(BF16))
         found = dot(chooser_t[h], jnp.concatenate(grads, axis=1), ((1,), (0,)))
         first = h * 3 * HS

time: 149 us -> 147 us (0.987)
  the two profiles are of different devices: /device:TPU:1 before, /device:TPU:2 now
where the time goes in v5:
time: 147 us
  Pallas kernels  147 us (100%)
    pallas_call x1, Pallas kernels, per_device(): pl.pallas_call(functools.partial(kernel, ny, nz), out_shape=shapes, in_sp...  145 us

profile of v5, /device:TPU:2, one launch (start us, length us, event | category | flops | bytes accessed | tf_op | source)
XLA Modules:
  0.0 147.2 jit_solution(14449289462250825270)
XLA Ops:
  0.6 144.8 %shard_map.68 = (bf16[256,768]{1,0:T(8,128)(2,1)}, f32[64,256]{1,0:T(8,128)}) custom-call(f32[2,128]{1,0:T(2,128)} %gain.1, s32[2,1,256]{2,1,0:T(1,128)} %bitcast.1, bf16[256,768]{1,0:T(8,128)(2,1)} %proj_in.1, bf16[256,4096]{1,0:T(8,128)(2,1)} %d_out_in.1, bf16[4096,256]{1,0:T(8,128)(2,1)} %w_out_in.1), custom_call_target="tpu_custom_call" | custom-call | tf_op jit(solution)/shard_map/pallas_call | solution.py:372
  145.5 1.8 %shard_map.69 = (bf16[256,768]{1,0:T(8,128)(2,1)}, f32[64,256]{1,0:T(8,128)}) custom-call(bf16[256,768]{1,0:T(8,128)(2,1)} %get-tuple-element.4.d_proj, f32[64,256]{1,0:T(8,128)} %get-tuple-element.5.d_w), custom_call_target="tpu_custom_call" | custom-call | tf_op jit(solution)/shard_map/pallas_call | solution.py:381

commit v6 on v5

--- a/solution.py
+++ b/solution.py
@@ -20,7 +20,7 @@
 OUT_BLOCKS = 5
 BACK = (((0, 0),), ((1, 0),), ((0, 1), (1, 1), (0, 2), (1, 2), (0, 3), (1, 3)))
 REST = (False, True, True)
-WEIGHTS = (0.15, 0.35, 0.15)
+WEIGHTS = (0.15, 0.3, 0.12)
 
 
 def dot(a, b, dims):
@@ -75,7 +75,7 @@
         j, dy = lax.div(step, ny), lax.rem(step, ny)
         dz = jnp.where(lax.rem(j, 2) == 1, lax.div(j + 1, 2), nz - lax.div(j, 2))
         if mirror:
-            dz = jnp.where(2 * dy < ny, dz, 2 * nz - dz)
+            dz = jnp.where(lax.rem(dy, 2) == 0, dz, 2 * nz - dz)
         return lax.rem(my_y + dy, ny) * nz + lax.rem(my_z + dz, nz)
 
     def along_y(dy):
@@ -135,7 +135,7 @@
     def block_of(message, i):
         return message[:, i * BLOCK:(i + 1) * BLOCK]
 
-    def to_all(src, dst, number, steps=(1, n), mirror=False):
+    def to_all(src, dst, number, steps=(1, n), mirror=True):
         @pl.loop(*steps)
         def _(step):
             target = other(step, mirror)

time: 147 us -> 146 us (level)
  the two profiles are of different devices: /device:TPU:2 before, /device:TPU:4 now
where the time goes in v6:
time: 146 us
  Pallas kernels  145 us (99%)
    pallas_call x1, Pallas kernels, per_device(): pl.pallas_call(functools.partial(kernel, ny, nz), out_shape=shapes, in_sp...  144 us

profile of v6, /device:TPU:4, one launch (start us, length us, event | category | flops | bytes accessed | tf_op | source)
XLA Modules:
  0.0 146.1 jit_solution(4808039449516764917)
XLA Ops:
  0.6 143.6 %shard_map.68 = (bf16[256,768]{1,0:T(8,128)(2,1)}, f32[64,256]{1,0:T(8,128)}) custom-call(f32[2,128]{1,0:T(2,128)} %gain.1, s32[2,1,256]{2,1,0:T(1,128)} %bitcast.1, bf16[256,768]{1,0:T(8,128)(2,1)} %proj_in.1, bf16[256,4096]{1,0:T(8,128)(2,1)} %d_out_in.1, bf16[4096,256]{1,0:T(8,128)(2,1)} %w_out_in.1), custom_call_target="tpu_custom_call" | custom-call | tf_op jit(solution)/shard_map/pallas_call | solution.py:372
  144.3 1.8 %shard_map.69 = (bf16[256,768]{1,0:T(8,128)(2,1)}, f32[64,256]{1,0:T(8,128)}) custom-call(bf16[256,768]{1,0:T(8,128)(2,1)} %get-tuple-element.4.d_proj, f32[64,256]{1,0:T(8,128)} %get-tuple-element.5.d_w), custom_call_target="tpu_custom_call" | custom-call | tf_op jit(solution)/shard_map/pallas_call | solution.py:381
